TPU v7x, 32 devices: a whole 2x2x4 slice. The times are simulated.
32 devices in a mesh: vis: 4 (over y, core), band: 8 (over z, x).
Axes of the slice: x: 2, y: 2, z: 4, core: 2. Of those that a mesh axis runs over, the one named last changes fastest.
Arguments:
- vis_values: float32 [2, 131072], P(None, ('vis', 'band')), may hold values from -6 to 6
- time_block: int32 [131072], P(('vis', 'band')), may hold values from 0 to 7
- block_gains: float32 [2, 8], replicated, may hold values from -4 to 4
- target_tile: int32 [131072, 1], P(('vis', 'band')), may hold values from 0 to 31; in each aligned block of 4096 rows (0 to 4095, 4096 to 8191, ...) at most 256 rows name the same one
- cell_row: int32 [131072], P(('vis', 'band')), may hold values from 0 to 1023
- cell_column: int32 [131072], P(('vis', 'band')), may hold values from 0 to 2047
- offsets: int32 [2, 131072], P(None, ('vis', 'band')), may hold values from 0 to 127
- kernel: float32 [128, 8], replicated, may hold values from 0.1 to 1
Outputs:
- sky_image: float32 [2, 8192, 8192], P(None, ('vis', 'band'))
Inputs may be any that keep to these rules, and one draw needn't show every extreme that they name: `target_tile`: among the visibilities of one device (aligned blocks of 4096 rows), no tile is named more than 256 times.
All inputs are finite; a program needn't handle non-finite values.
Results may differ from a plain program's by a relative error of at most 0.0038.
Values sent between devices are 32-bit elements; how exact they have to be, the bound alone decides.
A program may use at most 192 MiB of HBM per device.

v0:
```python
import math

import jax
import jax.numpy as jnp
from jax import lax
from jax.sharding import PartitionSpec as P

GRID = 8192


first_factor = 64
block_rows = 1024
highest = lax.Precision.HIGHEST


def shifted(value, axis, steps):
    count = lax.axis_size(axis)
    pairs = [(source, (source + steps) % count) for source in range(count)]
    return lax.ppermute(value, axis, pairs)


def phase_pair(products, modulus):
    phase_angle = 2.0 * math.pi / modulus * products.astype(jnp.float32)
    return (jnp.cos(phase_angle), jnp.sin(phase_angle))


def transform(paired):
    length = paired.shape[-1]
    line_count = paired.shape[1]
    second = length // first_factor
    arranged = paired.reshape(2, line_count, first_factor, second)
    outer_index = jnp.arange(first_factor, dtype=jnp.int32)
    inner_index = jnp.arange(second, dtype=jnp.int32)
    small_cos, small_sin = phase_pair(
        outer_index[:, None] * outer_index[None, :] % first_factor, first_factor
    )
    mixed_real = jnp.einsum("mab,ac->mcb", arranged[0], small_cos, precision=highest) - jnp.einsum(
        "mab,ac->mcb", arranged[1], small_sin, precision=highest
    )
    mixed_imag = jnp.einsum("mab,ac->mcb", arranged[1], small_cos, precision=highest) + jnp.einsum(
        "mab,ac->mcb", arranged[0], small_sin, precision=highest
    )
    twist_cos, twist_sin = phase_pair(outer_index[:, None] * inner_index[None, :] % length, length)
    turned_real = mixed_real * twist_cos - mixed_imag * twist_sin
    turned_imag = mixed_real * twist_sin + mixed_imag * twist_cos
    large_cos, large_sin = phase_pair(inner_index[:, None] * inner_index[None, :] % second, second)
    layout = "mcb,bd->mdc"
    out_real = jnp.einsum(layout, turned_real, large_cos, precision=highest) - jnp.einsum(
        layout, turned_imag, large_sin, precision=highest
    )
    out_imag = jnp.einsum(layout, turned_imag, large_cos, precision=highest) + jnp.einsum(
        layout, turned_real, large_sin, precision=highest
    )
    out_shape = (line_count, length)
    return jnp.stack([out_real.reshape(out_shape), out_imag.reshape(out_shape)])


def grid_block(running, portion, kernel, rows_padded, columns_padded, cols_block):
    values, indices = portion
    oversample = kernel.shape[0]
    support = kernel.shape[1]
    cell_index = indices[0]
    offset_index = indices[1]
    levels = jnp.arange(oversample, dtype=jnp.int32)[:, None]
    row_onehot = ((offset_index // oversample)[None, :] == levels).astype(jnp.float32)
    column_onehot = ((offset_index % oversample)[None, :] == levels).astype(jnp.float32)
    row_table = jnp.dot(kernel.T, row_onehot, precision=highest)
    column_table = jnp.dot(kernel.T, column_onehot, precision=highest)
    row_weights = (values[:, None, :] * row_table[None]).astype(jnp.bfloat16)
    column_weights = column_table.astype(jnp.bfloat16)
    row_reach = (
        jnp.arange(rows_padded, dtype=jnp.int32)[:, None] - (cell_index // cols_block)[None, :]
    )
    column_reach = (
        jnp.arange(columns_padded, dtype=jnp.int32)[:, None] - (cell_index % cols_block)[None, :]
    )
    width = values.shape[1]
    left_table = jnp.zeros((2, rows_padded, width), jnp.bfloat16)
    right_table = jnp.zeros((columns_padded, width), jnp.bfloat16)
    for placed in range(support):
        left_table = left_table + jnp.where(
            (row_reach == placed)[None], row_weights[:, placed][:, None, :], 0
        )
        right_table = right_table + jnp.where(
            column_reach == placed, column_weights[placed][None, :], 0
        )
    return running + jnp.einsum(
        "zur,cr->zcu", left_table, right_table, preferred_element_type=jnp.float32
    )


def local(vis_values, time_block, block_gains, target_tile, cell_row, cell_column, offsets, kernel):
    vis_devices = lax.axis_size("vis")
    band_devices = lax.axis_size("band")
    tile_count = vis_devices * band_devices
    held_count = vis_values.shape[1]
    capacity = 2 * held_count // tile_count
    grid_size = GRID
    rows_band = grid_size // band_devices
    cols_block = grid_size // vis_devices
    support = kernel.shape[1]
    oversample = kernel.shape[0]
    pick = time_block[None, :] == jnp.arange(block_gains.shape[1], dtype=jnp.int32)[:, None]
    gain_real = jnp.sum(jnp.where(pick, block_gains[0][:, None], 0.0), axis=0)
    gain_imag = jnp.sum(jnp.where(pick, block_gains[1][:, None], 0.0), axis=0)
    corrected_real = gain_real * vis_values[0] - gain_imag * vis_values[1]
    corrected_imag = gain_real * vis_values[1] + gain_imag * vis_values[0]
    packed_cell = (cell_row * cols_block + cell_column).astype(jnp.float32)
    packed_offset = (offsets[0] * oversample + offsets[1]).astype(jnp.float32)
    target = target_tile[:, 0]
    sorted_all = lax.sort(
        (target, corrected_real, corrected_imag, packed_cell, packed_offset),
        num_keys=1,
        is_stable=True,
    )
    sorted_target = sorted_all[0]
    position = jnp.arange(held_count, dtype=jnp.int32)
    starts_here = jnp.concatenate([jnp.ones((1,), bool), sorted_target[1:] != sorted_target[:-1]])
    segment_start = lax.cummax(jnp.where(starts_here, position, 0), axis=0)
    slot_index = sorted_target * capacity + (position - segment_start)
    sorted_rows = jnp.stack(sorted_all[1:])
    send_all = jnp.zeros((4, tile_count * capacity), jnp.float32).at[:, slot_index].set(sorted_rows)
    send_values = send_all[:2].reshape(2, vis_devices, band_devices * capacity)
    send_index = send_all[2:].astype(jnp.int32).reshape(2, vis_devices, band_devices * capacity)
    arrived = (
        lax.all_to_all(
            lax.all_to_all(send_values, "vis", split_axis=1, concat_axis=1, tiled=True),
            "band",
            split_axis=2,
            concat_axis=2,
            tiled=True,
        ),
        lax.all_to_all(
            lax.all_to_all(send_index, "vis", split_axis=1, concat_axis=1, tiled=True),
            "band",
            split_axis=2,
            concat_axis=2,
            tiled=True,
        ),
    )
    received_total = tile_count * capacity
    block_size = math.gcd(received_total, block_rows)
    block_total = received_total // block_size
    value_blocks = jnp.moveaxis(arrived[0].reshape(2, block_total, block_size), 1, 0)
    index_blocks = jnp.moveaxis(arrived[1].reshape(2, block_total, block_size), 1, 0)
    rows_padded = rows_band + support
    columns_padded = cols_block + support

    def scan_step(running, portion):
        return (grid_block(running, portion, kernel, rows_padded, columns_padded, cols_block), None)

    padded_tile, _ = lax.scan(
        scan_step,
        jnp.zeros((2, columns_padded, rows_padded), jnp.float32),
        (value_blocks, index_blocks),
    )
    column_spill = shifted(padded_tile[:, cols_block:, :], "vis", 1)
    main_tile = padded_tile[:, :cols_block, :].at[:, :support, :].add(column_spill)
    column_share = cols_block // band_devices
    row_spill = shifted(main_tile[:, :, rows_band:], "band", 1)
    core_tile = main_tile[:, :, :rows_band].at[:, :, :support].add(row_spill)
    spread = lax.all_to_all(core_tile, "band", split_axis=1, concat_axis=2, tiled=True)
    row_spectrum = transform(spread)
    gathered = lax.all_to_all(
        lax.all_to_all(row_spectrum, "vis", split_axis=2, concat_axis=1, tiled=True),
        "band",
        split_axis=2,
        concat_axis=1,
        tiled=True,
    )
    row_share = gathered.shape[2]
    ordered = gathered.reshape(2, band_devices, vis_devices, column_share, row_share)
    ordered = jnp.transpose(ordered, (0, 4, 2, 1, 3)).reshape(2, row_share, grid_size)
    sky_scale = 1.0 / (6.0 * math.sqrt(held_count * tile_count))
    return transform(ordered) * sky_scale


def solution(mesh):
    in_specs = (
        P(None, ("vis", "band")),
        P(("vis", "band")),
        P(),
        P(("vis", "band"), None),
        P(("vis", "band")),
        P(("vis", "band")),
        P(None, ("vis", "band")),
        P(),
    )
    out_specs = P(None, ("vis", "band"), None)
    return jax.shard_map(local, mesh=mesh, in_specs=in_specs, out_specs=out_specs, check_vma=False)
```

profile of v0, /device:TPU:0, one launch (start us, length us, event | category | flops | bytes accessed | tf_op | source)
XLA Modules:
  0.0 2010.8 jit_solution(446694599110201545)
XLA Ops:
  4.1 7.0 sort.47
  12.6 12.8 scatter_custom_fusion
  25.4 7.8 fusion.265
  53.3 6.5 all-to-all-start.1
  83.2 385.9 %while.16 = (s32[]{:T(128)}, f32[2,2056,1032]{1,2,0:T(8,128)}, s32[8,2,1024]{2,0,1:T(8,128)S(1)}, f32[128,8]{0,1:T(8,128)S(1)}, f32[8,2,1024]{2,0,1:T(8,128)S(1)}, /*index=5*/s32[]{:T(128)}, s32[]{:T(128)}, s32[]{}) while((s32[]{:T(128)}, f32[2,2056,1032]{1,2,0:T(8,128)}, s32[8,2,1024]{2,0,1:T(8,128)S(1)}, f32[128,8]{0,1:T(8,128)S(1)}, ...), condition=%wide.region_7.8_spmd.clone, body=%wide.region_6.7_spmd.clone.sunk | while | flops 8854566912 | bytes 51225716 | solution.py:152
  84.4 5.8 fusion.292
  90.2 39.9 %fusion.294 = f32[2,2056,1032]{1,2,0:T(8,128)} fusion(f32[2,2056,1032]{1,2,0:T(8,128)} %get-tuple-element.350, pred[]{:T(512)S(6)} %compare.55, pred[1032,1024]{1,0:T(8,128)(4,1)S(1)} %get-tuple-element.313, pred[1032,1024]{1,0:T(8,128)(4,1)S(1)} %get-tuple-element.314, pred[1032,1024]{1,0:T(8,128)(4,1)} %get-tuple-element.315, ...), kind=kOutput, calls=%fused_computation.2.clone.1 | convolution fusion | flops 8819548160 | bytes 42456064 | tf_op jit(solution)/shard_map/while/body/eval_jaxpr/zur,cr->zcu/dot_general | solution.py:87
  130.9 5.8 fusion.292
  136.7 41.8 %fusion.294 = f32[2,2056,1032]{1,2,0:T(8,128)} fusion(f32[2,2056,1032]{1,2,0:T(8,128)} %get-tuple-element.350, pred[]{:T(512)S(6)} %compare.55, pred[1032,1024]{1,0:T(8,128)(4,1)S(1)} %get-tuple-element.313, pred[1032,1024]{1,0:T(8,128)(4,1)S(1)} %get-tuple-element.314, pred[1032,1024]{1,0:T(8,128)(4,1)} %get-tuple-element.315, ...), kind=kOutput, calls=%fused_computation.2.clone.1 | convolution fusion | flops 8819548160 | bytes 42456064 | tf_op jit(solution)/shard_map/while/body/eval_jaxpr/zur,cr->zcu/dot_general | solution.py:87
  179.3 5.8 fusion.292
  185.1 41.8 %fusion.294 = f32[2,2056,1032]{1,2,0:T(8,128)} fusion(f32[2,2056,1032]{1,2,0:T(8,128)} %get-tuple-element.350, pred[]{:T(512)S(6)} %compare.55, pred[1032,1024]{1,0:T(8,128)(4,1)S(1)} %get-tuple-element.313, pred[1032,1024]{1,0:T(8,128)(4,1)S(1)} %get-tuple-element.314, pred[1032,1024]{1,0:T(8,128)(4,1)} %get-tuple-element.315, ...), kind=kOutput, calls=%fused_computation.2.clone.1 | convolution fusion | flops 8819548160 | bytes 42456064 | tf_op jit(solution)/shard_map/while/body/eval_jaxpr/zur,cr->zcu/dot_general | solution.py:87
  227.7 5.8 fusion.292
  233.5 41.8 %fusion.294 = f32[2,2056,1032]{1,2,0:T(8,128)} fusion(f32[2,2056,1032]{1,2,0:T(8,128)} %get-tuple-element.350, pred[]{:T(512)S(6)} %compare.55, pred[1032,1024]{1,0:T(8,128)(4,1)S(1)} %get-tuple-element.313, pred[1032,1024]{1,0:T(8,128)(4,1)S(1)} %get-tuple-element.314, pred[1032,1024]{1,0:T(8,128)(4,1)} %get-tuple-element.315, ...), kind=kOutput, calls=%fused_computation.2.clone.1 | convolution fusion | flops 8819548160 | bytes 42456064 | tf_op jit(solution)/shard_map/while/body/eval_jaxpr/zur,cr->zcu/dot_general | solution.py:87
  276.1 5.8 fusion.292
  281.9 41.8 %fusion.294 = f32[2,2056,1032]{1,2,0:T(8,128)} fusion(f32[2,2056,1032]{1,2,0:T(8,128)} %get-tuple-element.350, pred[]{:T(512)S(6)} %compare.55, pred[1032,1024]{1,0:T(8,128)(4,1)S(1)} %get-tuple-element.313, pred[1032,1024]{1,0:T(8,128)(4,1)S(1)} %get-tuple-element.314, pred[1032,1024]{1,0:T(8,128)(4,1)} %get-tuple-element.315, ...), kind=kOutput, calls=%fused_computation.2.clone.1 | convolution fusion | flops 8819548160 | bytes 42456064 | tf_op jit(solution)/shard_map/while/body/eval_jaxpr/zur,cr->zcu/dot_general | solution.py:87
  330.3 41.8 %fusion.294 = f32[2,2056,1032]{1,2,0:T(8,128)} fusion(f32[2,2056,1032]{1,2,0:T(8,128)} %get-tuple-element.350, pred[]{:T(512)S(6)} %compare.55, pred[1032,1024]{1,0:T(8,128)(4,1)S(1)} %get-tuple-element.313, pred[1032,1024]{1,0:T(8,128)(4,1)S(1)} %get-tuple-element.314, pred[1032,1024]{1,0:T(8,128)(4,1)} %get-tuple-element.315, ...), kind=kOutput, calls=%fused_computation.2.clone.1 | convolution fusion | flops 8819548160 | bytes 42456064 | tf_op jit(solution)/shard_map/while/body/eval_jaxpr/zur,cr->zcu/dot_general | solution.py:87
  378.7 41.8 %fusion.294 = f32[2,2056,1032]{1,2,0:T(8,128)} fusion(f32[2,2056,1032]{1,2,0:T(8,128)} %get-tuple-element.350, pred[]{:T(512)S(6)} %compare.55, pred[1032,1024]{1,0:T(8,128)(4,1)S(1)} %get-tuple-element.313, pred[1032,1024]{1,0:T(8,128)(4,1)S(1)} %get-tuple-element.314, pred[1032,1024]{1,0:T(8,128)(4,1)} %get-tuple-element.315, ...), kind=kOutput, calls=%fused_computation.2.clone.1 | convolution fusion | flops 8819548160 | bytes 42456064 | tf_op jit(solution)/shard_map/while/body/eval_jaxpr/zur,cr->zcu/dot_general | solution.py:87
  427.1 41.8 %fusion.294 = f32[2,2056,1032]{1,2,0:T(8,128)} fusion(f32[2,2056,1032]{1,2,0:T(8,128)} %get-tuple-element.350, pred[]{:T(512)S(6)} %compare.55, pred[1032,1024]{1,0:T(8,128)(4,1)S(1)} %get-tuple-element.313, pred[1032,1024]{1,0:T(8,128)(4,1)S(1)} %get-tuple-element.314, pred[1032,1024]{1,0:T(8,128)(4,1)} %get-tuple-element.315, ...), kind=kOutput, calls=%fused_computation.2.clone.1 | convolution fusion | flops 8819548160 | bytes 42456064 | tf_op jit(solution)/shard_map/while/body/eval_jaxpr/zur,cr->zcu/dot_general | solution.py:87
  469.1 20.0 copy.151
  489.9 12.0 slice.261
  503.2 7.8 scatter-add.6
  512.6 11.8 slice.311
  526.0 25.4 %copy.154 = f32[2,2048,1024]{2,0,1:T(2,128)} copy(f32[2,2048,1024]{1,2,0:T(8,128)} %fusion.133) | data formatting | bytes 33554432 | tf_op jit(solution)/shard_map/scatter-add | solution.py:161
  557.4 363.6 %all-to-all-done.4 = f32[2,2048,1024]{2,0,1:T(2,128)} async-done(((f32[2,2048,1024]{2,0,1:T(2,128)}), f32[2,2048,1024]{2,0,1:T(2,128)}, u32[]{:S(2)}, u32[]{:S(2)}) %all-to-all-start.4) | async-done | bytes 16777248 | tf_op jit(solution)/shard_map/all_to_all | solution.py:162
  921.0 15.2 copy.208
  936.2 6.7 fusion.264
  943.0 9.3 squeeze.43
  952.2 12.7 fusion.160
  964.9 10.2 fusion.166
  975.1 9.3 squeeze.42
  984.4 11.9 fusion.158
  996.3 19.6 subtract_bitcast_fusion.3
  1015.9 18.4 fusion.117
  1034.4 12.9 fusion.115
  1047.4 19.3 subtract_bitcast_fusion.2
  1066.7 11.5 copy.158
  1078.1 17.9 add_bitcast_fusion.2
  1096.1 11.5 copy.161
  1107.5 6.5 pad_maximum_fusion
  1114.0 46.1 %copy.162 = f32[2,256,8192]{1,0,2:T(2,128)} copy(f32[2,256,8192]{1,2,0:T(8,128)S(1)} %pad_maximum_fusion) | data formatting | bytes 33554432 | tf_op jit(solution)/shard_map/stack | solution.py:55
  1160.1 187.7 %all_to_all.68 = f32[2,256,8192]{1,0,2:T(2,128)S(1)} all-to-all(f32[2,256,8192]{1,0,2:T(2,128)} %copy.162), channel_id=1, replica_groups=mesh['vis'=4,'band'=8] {'vis'}, dimensions={2} | all-to-all | bytes 33554432 | tf_op jit(solution)/shard_map/all_to_all | solution.py:165
  1347.8 8.3 copy.163
  1356.1 16.5 copy.164
  1372.6 25.3 %copy.165 = f32[2,1024,2048]{1,0,2:T(2,128)} copy(f32[2,1024,2048]{2,1,0:T(8,128)} %bitcast.187) | data formatting | bytes 33554432 | tf_op jit(solution)/shard_map/all_to_all | solution.py:165
  1397.9 367.0 %all_to_all.69 = f32[2,1024,2048]{1,0,2:T(2,128)S(1)} all-to-all(f32[2,1024,2048]{1,0,2:T(2,128)} %copy.165), channel_id=1, replica_groups=mesh['vis'=4,'band'=8] {'band'}, dimensions={2} | all-to-all | bytes 33554432 | tf_op jit(solution)/shard_map/all_to_all | solution.py:164
  1764.9 11.9 copy.166
  1776.9 17.3 copy.167
  1794.2 11.3 fusion.263
  1805.5 10.5 copy.169
  1815.9 9.0 squeeze.45
  1824.9 12.7 fusion.156
  1837.6 9.7 fusion.162
  1847.3 10.7 copy.168
  1858.0 8.9 squeeze.44
  1866.9 11.9 fusion.154
  1878.8 19.8 subtract_bitcast_fusion.1
  1898.6 18.6 fusion.109
  1917.2 12.7 fusion.107
  1930.0 19.3 subtract_bitcast_fusion
  1949.3 11.5 copy.172
  1960.8 17.9 add_bitcast_fusion
  1978.7 8.4 copy.175
  1987.1 6.1 maximum_multiply_fusion
  1993.2 17.5 copy.176
  (164 shorter events, 83.5 us)
Async XLA Ops:
  36.7 8.4 all-to-all-start
  45.1 8.2 all-to-all-start.2
  49.5 33.7 %copy-start.9 = (f32[128,8]{0,1:T(8,128)S(1)}, f32[128,8]{0,1:T(8,128)}, u32[]{:S(2)}) copy-start(f32[128,8]{0,1:T(8,128)} %param.21) | copy-start | bytes 12292
  53.3 13.4 all-to-all-start.1
  66.7 11.0 all-to-all-start.3
  489.9 12.0 collective-permute-start
  511.9 12.5 collective-permute-start.1
  551.4 369.6 %all-to-all-start.4 = ((f32[2,2048,1024]{2,0,1:T(2,128)}), f32[2,2048,1024]{2,0,1:T(2,128)}, u32[]{:S(2)}, u32[]{:S(2)}) async-start(f32[2,2048,1024]{2,0,1:T(2,128)} %copy.154), calls=%async_computation.4 | async-start | bytes 33554432 | tf_op jit(solution)/shard_map/all_to_all | solution.py:162
  557.3 438.9 %copy-start.5 = (f32[64,128]{1,0:T(8,128)}, f32[64,128]{1,0:T(8,128)S(1)}, u32[]{:S(2)}) copy-start(f32[64,128]{1,0:T(8,128)S(1)} %get-tuple-element.248) | copy-start | bytes 98308
  557.3 438.9 %copy-start.7 = (f32[64,128]{1,0:T(8,128)}, f32[64,128]{1,0:T(8,128)S(1)}, u32[]{:S(2)}) copy-start(f32[64,128]{1,0:T(8,128)S(1)} %get-tuple-element.249) | copy-start | bytes 98308
  952.2 12.7 copy-start
  1015.9 18.5 copy-start.3
  1015.9 31.4 %slice-start.2 = ((s8[8388608]{0:T(1024)(128)(4,1)}), s8[4194304]{0:T(1024)(128)(4,1)S(1)}, s32[]{:S(2)}) async-start(s8[8388608]{0:T(1024)(128)(4,1)} %bitcast.182), calls=%async_computation.9 | async-start | bytes 8388608
  1034.4 13.0 slice-start.3
  1824.9 12.7 copy-start.1
  1866.9 11.9 copy-start.6
  1866.9 11.9 copy-start.8
  1898.6 18.6 copy-start.2
  1898.6 31.4 %slice-start = ((s8[8388608]{0:T(1024)(128)(4,1)}), s8[4194304]{0:T(1024)(128)(4,1)S(1)}, s32[]{:S(2)}) async-start(s8[8388608]{0:T(1024)(128)(4,1)} %bitcast.180), calls=%async_computation.7 | async-start | bytes 8388608
  1917.2 12.7 slice-start.1
  1978.7 8.4 copy-start.4
where the time goes:
time: 2020 us; the launch traced here: 2010 us
  matrix products  582 us (29%)
  blocking collectives  555 us (27%)
  local copies, waits for them, and re-layouts  398 us (20%)
  waiting for transfers between devices  368 us (18%)
  other arithmetic  81.6 us (4%)
  starting transfers between devices  24.5 us (1%)
    all_to_all x1, blocking collectives, local(): lax.all_to_all(lax.all_to_all(row_spectrum, 'vis', split_axis=2, concat_a...  367 us
    all_to_all x1, waiting for transfers between devices, local(): lax.all_to_all(core_tile, 'band', split_axis=1, concat_axis=2, tiled=True)  364 us
    dot_general x8, matrix products, grid_block(): jnp.einsum('zur,cr->zcu', left_table, right_table, preferred_element_type...  332 us
    all_to_all x1, blocking collectives, local(): lax.all_to_all(row_spectrum, 'vis', split_axis=2, concat_axis=1, tiled=True)  188 us
    all_to_all x3, local copies, waits for them, and re-layouts, local(): lax.all_to_all(row_spectrum, 'vis', split_axis=2, concat_axis=1, tiled=True)  50 us
    eq x8, other arithmetic, grid_block(): row_reach == placed  46.5 us
    another operation x1, local copies, waits for them, and re-layouts, transform(): return jnp.stack([out_real.reshape(out_shape), out_imag.reshape(out_shape)])  46.1 us
  transfers between devices with their start and end apart: 7, of which 4 were waited for; matrix products, arithmetic and copies ran while one was open for 2% of the time, Pallas kernels for 0%

commit v1 on v0

v1 whole, which is shorter than its diff:
```python
import math

import jax
import jax.numpy as jnp
from jax import lax
from jax.experimental import pallas as pl
from jax.experimental.pallas import tpu as pltpu
from jax.sharding import PartitionSpec as P

GRID = 8192
CHUNK = 256
WINDOW = 256
ALIGN = 128
ROW_STEP = 64
GATHERED = 131072
FIRST = 128


def phase_pair(products, modulus):
    phase_angle = 2.0 * math.pi / modulus * (products % modulus).astype(jnp.float32)
    return (jnp.cos(phase_angle), jnp.sin(phase_angle))


def spread_cyclic(table, shift):
    for bit in (1, 2, 4):
        table = jnp.where((shift & bit) != 0, pltpu.roll(table, bit, 0), table)
    return table


def grid_kernel(low_ref, count_ref, data_ref, taps_ref, fine_ref, coarse_ref, acc_ref, left_ref):
    total = data_ref.shape[1]
    rows = fine_ref.shape[0] // 2
    distinct = coarse_ref.shape[0] // 2
    support = taps_ref.shape[0] // 4
    levels = taps_ref.shape[1]
    reach_rows = fine_ref.shape[1] // 2

    def clear(step, carry):
        acc_ref[pl.ds(pl.multiple_of(step * ALIGN, ALIGN), ALIGN), :] = jnp.zeros(
            (ALIGN, acc_ref.shape[1]), jnp.float32
        )
        return carry

    lax.fori_loop(0, acc_ref.shape[0] // ALIGN, clear, 0)

    def chunk(step, carry):
        data = data_ref[:, pl.ds(pl.multiple_of(step * CHUNK, CHUNK), CHUNK)]
        whole = data[2:6].astype(jnp.int32)
        row, column, row_offset, column_offset = (whole[k : k + 1] for k in range(4))
        level = lax.broadcasted_iota(jnp.int32, (levels, CHUNK), 0)
        row_hot = jnp.where(level == row_offset, 1.0, 0.0).astype(jnp.bfloat16)
        column_hot = jnp.where(level == column_offset, 1.0, 0.0).astype(jnp.bfloat16)
        row_taps = jnp.dot(taps_ref[...], row_hot, preferred_element_type=jnp.float32)
        column_taps = jnp.dot(taps_ref[...], column_hot, preferred_element_type=jnp.float32)
        row_taps = (row_taps[:support] + row_taps[support : 2 * support]) + row_taps[
            2 * support : 3 * support
        ]
        row_taps = spread_cyclic(row_taps, row & 7)
        column_taps = spread_cyclic(column_taps[3 * support :], column & 7)
        fine = row & (ROW_STEP - 1)
        reach = lax.broadcasted_iota(jnp.int32, (reach_rows, CHUNK), 0) - fine
        inside = (reach >= 0) & (reach < support)
        placed = []
        for part in range(2):
            weights = (data[part : part + 1] * row_taps).astype(jnp.bfloat16).astype(jnp.float32)
            tiled = jnp.concatenate([weights] * (reach_rows // support), axis=0)
            placed.append(jnp.where(inside, tiled, 0.0))
        placed = jnp.concatenate(placed, axis=0).astype(jnp.bfloat16)
        turned = jnp.dot(fine_ref[...], placed, preferred_element_type=jnp.float32)
        coarse_level = lax.broadcasted_iota(jnp.int32, (GRID // ROW_STEP, CHUNK), 0)
        coarse_hot = jnp.where(coarse_level == row // ROW_STEP, 1.0, 0.0).astype(jnp.bfloat16)
        coarse_hot = jnp.concatenate([coarse_hot, coarse_hot], axis=0)
        phase = jnp.dot(coarse_ref[...], coarse_hot, preferred_element_type=jnp.float32)
        phase_cos, phase_sin = phase[:distinct], phase[distinct:]
        for part in range(rows // distinct):
            real = turned[part * distinct : (part + 1) * distinct]
            imag = turned[rows + part * distinct : rows + (part + 1) * distinct]
            left_ref[part * distinct : (part + 1) * distinct, :] = (
                real * phase_cos - imag * phase_sin
            ).astype(jnp.bfloat16)
            left_ref[rows + part * distinct : rows + (part + 1) * distinct, :] = (
                real * phase_sin + imag * phase_cos
            ).astype(jnp.bfloat16)
        low = low_ref[step]

        def window(number, inner):
            base = pl.multiple_of(low + number * WINDOW, ALIGN)
            ahead = lax.broadcasted_iota(jnp.int32, (WINDOW, CHUNK), 0) - (column - base)
            tiled = jnp.concatenate([column_taps] * (WINDOW // support), axis=0)
            right = jnp.where((ahead >= 0) & (ahead < support), tiled, 0.0).astype(jnp.bfloat16)
            acc_ref[pl.ds(base, WINDOW), :] += lax.dot_general(
                right,
                left_ref[...],
                (((1,), (1,)), ((), ())),
                preferred_element_type=jnp.float32,
            )
            return inner

        lax.fori_loop(0, count_ref[step], window, 0)
        return carry

    lax.fori_loop(0, total // CHUNK, chunk, 0)
    acc_ref[:support, :] += acc_ref[GRID : GRID + support, :]


def grid_rows(data, taps, fine_table, coarse_table):
    columns = data[3].astype(jnp.int32).reshape(-1, CHUNK)
    low = jnp.min(columns, axis=1) // ALIGN * ALIGN
    support = taps.shape[0] // 4
    count = (jnp.max(columns, axis=1) + support - 1 - low) // WINDOW + 1
    width = fine_table.shape[0]
    in_smem = pl.BlockSpec(memory_space=pltpu.SMEM)
    in_vmem = pl.BlockSpec(memory_space=pltpu.VMEM)
    return pl.pallas_call(
        grid_kernel,
        out_shape=jax.ShapeDtypeStruct((GRID + WINDOW, width), jnp.float32),
        in_specs=[in_smem] * 2 + [in_vmem] * 4,
        out_specs=in_vmem,
        scratch_shapes=[pltpu.VMEM((width, CHUNK), jnp.bfloat16)],
        compiler_params=pltpu.CompilerParams(vmem_limit_bytes=48 * 1024 * 1024),
        name="grid_rows",
    )(low, count, data, taps, fine_table, coarse_table)


def transform_columns(columns, rows, scale):
    second = GRID // FIRST
    first_index = jnp.arange(FIRST, dtype=jnp.int32)
    second_index = jnp.arange(second, dtype=jnp.int32)
    arranged = columns.reshape(FIRST, second, 2 * rows)
    table = jnp.concatenate(
        phase_pair(first_index[:, None] * first_index[None, :], FIRST), axis=1
    )
    mixed = jnp.einsum("vk,vwx->kwx", table, arranged, precision=lax.Precision.HIGH)
    real = mixed[:FIRST, :, :rows] - mixed[FIRST:, :, rows:]
    imag = mixed[FIRST:, :, :rows] + mixed[:FIRST, :, rows:]
    twist_cos, twist_sin = phase_pair(first_index[:, None] * second_index[None, :], GRID)
    twist_cos, twist_sin = twist_cos[:, :, None], twist_sin[:, :, None]
    turned = jnp.concatenate(
        [real * twist_cos - imag * twist_sin, real * twist_sin + imag * twist_cos], axis=2
    )
    table = jnp.concatenate(
        phase_pair(second_index[:, None] * second_index[None, :], second), axis=1
    )
    mixed = jnp.einsum("wk,qwx->kqx", table, turned, precision=lax.Precision.HIGH)
    real = mixed[:second, :, :rows] - mixed[second:, :, rows:]
    imag = mixed[second:, :, :rows] + mixed[:second, :, rows:]
    image = jnp.stack([real, imag]) * scale
    return jnp.transpose(image, (0, 3, 1, 2)).reshape(2, rows, GRID)


def local(vis_values, time_block, block_gains, target_tile, cell_row, cell_column, offsets, kernel):
    vis_devices = lax.axis_size("vis")
    band_devices = lax.axis_size("band")
    devices = vis_devices * band_devices
    held_count = vis_values.shape[1]
    rows_band = GRID // band_devices
    cols_block = GRID // vis_devices
    rows = GRID // devices
    support = kernel.shape[1]
    oversample = kernel.shape[0]
    pick = time_block[None, :] == jnp.arange(block_gains.shape[1], dtype=jnp.int32)[:, None]
    gain_real = jnp.sum(jnp.where(pick, block_gains[0][:, None], 0.0), axis=0)
    gain_imag = jnp.sum(jnp.where(pick, block_gains[1][:, None], 0.0), axis=0)
    corrected_real = gain_real * vis_values[0] - gain_imag * vis_values[1]
    corrected_imag = gain_real * vis_values[1] + gain_imag * vis_values[0]
    target = target_tile[:, 0]
    first_row = target % band_devices * rows_band + cell_row
    first_column = target // band_devices * cols_block + cell_column
    cell, offset, corrected_real, corrected_imag = lax.sort(
        (
            first_column * GRID + first_row,
            offsets[0] * oversample + offsets[1],
            corrected_real,
            corrected_imag,
        ),
        num_keys=1,
        is_stable=False,
    )
    held = jnp.stack(
        [corrected_real, corrected_imag]
        + [
            index.astype(jnp.float32)
            for index in (cell % GRID, cell // GRID, offset // oversample, offset % oversample)
        ]
    )

    taps = kernel.T
    split, rest = [], taps
    for _ in range(3):
        split.append(lax.reduce_precision(rest, 8, 7))
        rest = rest - split[-1]
    taps = jnp.concatenate(split + [split[0]]).astype(jnp.bfloat16)

    own = (lax.axis_index("vis") * band_devices + lax.axis_index("band")) * rows
    row_index = own + jnp.arange(rows, dtype=jnp.int32)
    reach = jnp.arange(ROW_STEP + support, dtype=jnp.int32)
    fine_cos, fine_sin = phase_pair(row_index[:, None] * reach[None, :], GRID)
    fine_table = jnp.concatenate(
        [
            jnp.concatenate([fine_cos, -fine_sin], axis=1),
            jnp.concatenate([fine_sin, fine_cos], axis=1),
        ]
    ).astype(jnp.bfloat16)
    coarse_count = GRID // ROW_STEP
    distinct = min(rows, coarse_count)
    coarse_table = jnp.concatenate(
        phase_pair(
            row_index[:distinct, None] * jnp.arange(coarse_count, dtype=jnp.int32)[None, :],
            coarse_count,
        )
    )
    coarse_high = lax.reduce_precision(coarse_table, 8, 7)
    coarse_table = jnp.concatenate([coarse_high, coarse_table - coarse_high], axis=1).astype(
        jnp.bfloat16
    )

    pieces = max(1, held_count * devices // GATHERED)
    piece = held_count // pieces

    def grid_piece(part):
        data = lax.all_gather(part, ("vis", "band"), axis=1, tiled=True)
        return grid_rows(data, taps, fine_table, coarse_table)

    if pieces == 1:
        gridded = grid_piece(held)
    else:
        parts = jnp.moveaxis(held.reshape(held.shape[0], pieces, piece), 1, 0)
        gridded, _ = lax.scan(
            lambda running, part: (running + grid_piece(part), None),
            jnp.zeros((GRID + WINDOW, 2 * rows), jnp.float32),
            parts,
        )
    sky_scale = 1.0 / (6.0 * math.sqrt(held_count * devices))
    return transform_columns(gridded[:GRID], rows, sky_scale)


def solution(mesh):
    in_specs = (
        P(None, ("vis", "band")),
        P(("vis", "band")),
        P(),
        P(("vis", "band"), None),
        P(("vis", "band")),
        P(("vis", "band")),
        P(None, ("vis", "band")),
        P(),
    )
    out_specs = P(None, ("vis", "band"), None)
    return jax.shard_map(local, mesh=mesh, in_specs=in_specs, out_specs=out_specs, check_vma=False)
```

time: 2020 us -> 882 us (0.44)
  Pallas kernels: 0 us -> 612 us
  blocking collectives: 555 us -> 0 us
  matrix products: 582 us -> 78.5 us
  local copies, waits for them, and re-layouts: 398 us -> 53.5 us
  waiting for transfers between devices: 368 us -> 62.5 us
  starting transfers between devices: 24.5 us -> 0.01 us
  other arithmetic: 81.6 us -> 59 us
    pallas_call x0 -> x1, Pallas kernels: none -> 612 us  [grid_rows(): pl.pallas_call(grid_kernel, out_shape=jax.ShapeDtypeStruct((GRID + WINDOW...]
    all_to_all x2 -> x0, blocking collectives: 555 us -> none  [the longest x1 367 us: local(): lax.all_to_all(lax.all_to_all(row_spectrum, 'vis', split_axis=2, concat_a...]
    dot_general x40 -> x2, matrix products: 582 us -> 78.5 us  [the longest x1 44.6 us: transform_columns(): jnp.einsum('vk,vwx->kwx', table, arranged, precision=lax.Precision.HIGH)]
    all_to_all x5 -> x0, waiting for transfers between devices: 368 us -> none  [the longest x1 364 us: local(): lax.all_to_all(core_tile, 'band', split_axis=1, concat_axis=2, tiled=True)]
    all_to_all x12 -> x0, local copies, waits for them, and re-layouts: 99.6 us -> none  [the longest x3 50 us: local(): lax.all_to_all(row_spectrum, 'vis', split_axis=2, concat_axis=1, tiled=True)]
    all_gather x0 -> x1, waiting for transfers between devices: none -> 62.5 us  [grid_piece(): data = lax.all_gather(part, ('vis', 'band'), axis=1, tiled=True)]
    slice x24 -> x2, local copies, waits for them, and re-layouts: 65.7 us -> 11.7 us  [the longest x1 11.7 us: local(): return transform_columns(gridded[:GRID], rows, sky_scale)]
    eq x8 -> x0, other arithmetic: 46.5 us -> none  [grid_block(): row_reach == placed]
  transfers between devices with their start and end apart: 7 -> 1, of which waited for: 4 -> 1; matrix products, arithmetic and copies ran while one was open for 2% -> 0% of each run, Pallas kernels for 0% -> 0%
where the time goes in v1:
time: 882 us; the launch traced here: 880 us
  Pallas kernels  612 us (69%)
  matrix products  78.5 us (9%)
  waiting for transfers between devices  62.5 us (7%)
  other arithmetic  59 us (7%)
  local copies, waits for them, and re-layouts  53.5 us (6%)
  between operations  14 us (2%)
    pallas_call x1, Pallas kernels, grid_rows(): pl.pallas_call(grid_kernel, out_shape=jax.ShapeDtypeStruct((GRID + WINDOW...  612 us
    all_gather x1, waiting for transfers between devices, grid_piece(): data = lax.all_gather(part, ('vis', 'band'), axis=1, tiled=True)  62.5 us
    dot_general x1, matrix products, transform_columns(): jnp.einsum('vk,vwx->kwx', table, arranged, precision=lax.Precision.HIGH)  44.6 us
    dot_general x1, matrix products, transform_columns(): jnp.einsum('wk,qwx->kqx', table, turned, precision=lax.Precision.HIGH)  33.9 us
    another operation x1, other arithmetic, transform_columns(): image = jnp.stack([real, imag]) * scale  19.7 us
    transpose x1, local copies, waits for them, and re-layouts, transform_columns(): return jnp.transpose(image, (0, 3, 1, 2)).reshape(2, rows, GRID)  19.6 us
  transfers between devices with their start and end apart: 1, of which 1 were waited for; matrix products, arithmetic and copies ran while one was open for 0% of the time, Pallas kernels for 0%

profile of v1, /device:TPU:0, one launch (start us, length us, event | category | flops | bytes accessed | tf_op | source)
XLA Modules:
  0.0 879.7 jit_solution(4708539590743124267)
XLA Ops:
  6.5 0.0 all-gather.2.cloned.1.call-start
  6.5 0.8 slice_bitcast_fusion
  7.3 0.9 fusion.83
  8.2 0.9 slice_add_fusion.2
  9.0 0.9 select_reduce_fusion.1
  9.9 0.8 fusion.52
  10.7 5.0 sort.27
  15.8 0.8 stack.36
  16.6 0.0 all-gather.2.cloned.1.call-update
  16.6 0.7 reduce-precision_convert_fusion.1
  17.3 0.1 fusion.59
  17.5 0.1 fusion.63
  17.6 0.3 fusion.41
  17.9 0.3 fusion.44
  18.3 0.6 negate_convert_fusion
  18.9 0.1 maximum_maximum_fusion.fine_ref
  19.0 62.5 %all-gather.2.cloned.1.call-done.data_ref = f32[6,131072]{1,0:T(8,128)} async-done(((f32[6,4096]{1,0:T(8,128)}), f32[6,131072]{1,0:T(8,128)}) %all-gather.2.cloned.1.call-update) | async-done | bytes 3145744 | tf_op jit(solution)/shard_map/all_gather | solution.py:221
  81.5 3.9 fusion.7
  85.5 0.1 convert_element_type.69
  85.6 0.2 fusion.81
  85.9 0.0 copy-start
  85.9 2.2 copy-done
  88.1 612.1 %grid_rows.1 = f32[8448,512]{1,0:T(8,128)} custom-call(s32[512]{0:T(512)S(1)} %get-tuple-element.18.low_ref, s32[512]{0:T(512)S(1)} %get-tuple-element.17.count_ref, f32[6,131072]{1,0:T(8,128)S(1)} %copy-done, bf16[32,128]{1,0:T(8,128)(2,1)S(1)} %pad_maximum_fusion.3.taps_ref, bf16[512,144]{1,0:T(8,128)(2,1)S(1)} %maximum_maximum_fusion.fine_ref, ...), custom_call_target="tpu_custom_call" | custom-call | tf_op jit(solution)/shard_map/grid_rows/pallas_call | solution.py:114
  700.2 11.7 %slice.71 = f32[8192,512]{1,0:T(8,128)} slice(f32[8448,512]{1,0:T(8,128)} %grid_rows.1), slice={[0:8192], [0:512]} | slice | bytes 33554432 | tf_op jit(solution)/shard_map/slice | solution.py:234
  711.9 44.6 %fusion.3 = f32[256,64,512]{2,0,1:T(8,128)} fusion(f32[128,64,512]{2,1,0:T(8,128)} %bitcast.35, f32[128,128]{1,0:T(8,128)S(1)} %get-tuple-element.45, f32[128,128]{1,0:T(8,128)S(1)} %get-tuple-element.46), kind=kOutput, calls=%fused_computation.5 | convolution fusion | flops 6442483712 | bytes 50462720 | tf_op jit(solution)/shard_map/vk,vwx->kwx/dot_general | solution.py:133
  756.6 11.9 %multiply_subtract_fusion = (f32[128,64,256]{2,0,1:T(8,128)S(1)}, f32[128,64,256]{2,0,1:T(8,128)S(1)}) fusion(f32[128,64]{0,1:T(8,128)S(1)} %get-tuple-element.47, f32[128,64]{0,1:T(8,128)S(1)} %get-tuple-element.48, f32[256,64,512]{2,0,1:T(8,128)} %fusion.3), kind=kLoop, calls=%fused_computation.14 | loop fusion | flops 16777216 | bytes 50397184 | tf_op jit(solution)/shard_map/sub | solution.py:139
  768.4 6.5 pad_maximum_fusion
  774.9 33.9 %fusion.1 = f32[128,128,512]{2,0,1:T(8,128)} fusion(f32[128,64,512]{2,0,1:T(8,128)} %pad_maximum_fusion, f32[64,64]{1,0:T(8,128)S(1)} %get-tuple-element.49, f32[64,64]{1,0:T(8,128)S(1)} %get-tuple-element.50), kind=kOutput, calls=%fused_computation.3 | convolution fusion | flops 3221233664 | bytes 50364416 | tf_op jit(solution)/shard_map/wk,qwx->kqx/dot_general | solution.py:144
  808.8 19.7 %fusion.6 = (f32[1,64,128,256]{3,1,2,0:T(8,128)}, f32[1,64,128,256]{3,1,2,0:T(8,128)}) fusion(f32[128,128,512]{2,0,1:T(8,128)} %fusion.1), kind=kLoop, calls=%fused_computation.10 | loop fusion | flops 4194304 | bytes 50331648 | tf_op jit(solution)/shard_map/stack | solution.py:147
  828.6 6.8 fusion
  835.3 19.6 %copy.20 = f32[2,256,64,128]{1,3,2,0:T(8,128)} copy(f32[2,256,64,128]{1,2,3,0:T(8,128)S(1)} %fusion) | data formatting | bytes 33554432 | tf_op jit(solution)/shard_map/transpose | solution.py:148
  854.9 17.5 %copy.21 = f32[2,256,8192]{2,1,0:T(8,128)} copy(f32[2,256,8192]{1,2,0:T(8,128)} %bitcast.36) | data formatting | bytes 33554432 | tf_op jit(solution)/shard_map/reshape | solution.py:148
  (8 shorter events, 0.1 us)
Async XLA Ops:
  6.5 75.0 %all-gather.2.cloned.1.call-start = ((), (), s32[]{:S(2)}) async-start(), calls=%async_computation | async-start | bytes 4325376 | tf_op jit(solution)/shard_map/all_gather | solution.py:221
  85.9 2.2 copy-start
Sparse Core Ops, SparseCore 0:
  16.7 64.7 all-gather.1
